TPU v7x, 128 devices: a whole 4x4x4 slice. The times are simulated.
128 devices in a mesh: emit: 8 (over x_hi, z), elem: 16 (over y, x_lo, core).
Axes of the slice: x: 4 (x_hi: 2, x_lo: 2; x = x_hi * 2 + x_lo), y: 4, z: 4, core: 2. Of those that a mesh axis runs over, the one named last changes fastest.
Arguments:
- traces: float32 [256, 1024, 1024], P('emit', 'elem'), may hold values from -6 to 6
- codes: float32 [4, 2, 128], replicated, may hold values from -0.5 to 0.5
- code_of: int32 [256], replicated, may hold values from 0 to 3
- order: int32 [256], replicated, may hold values from 0 to 255, each once
- steer: float32 [256, 1024, 256], P(None, 'elem'), may hold values from -0.1875 to 0.1875
Outputs:
- beams: float32 [256, 256, 256], P('elem', 'emit')
Inputs may be any that keep to these rules, and one draw needn't show every extreme that they name: `order`: each value 0 to 255 appears exactly once.
All inputs are finite; a program needn't handle non-finite values.
Results may differ from a plain program's by a relative error of at most 0.000071.
Values sent between devices are 32-bit elements; how exact they have to be, the bound alone decides.
A program may use at most 192 MiB of HBM per device.

v0:
```python
import jax
import jax.numpy as jnp
from jax import lax
from jax.sharding import PartitionSpec as P


def toeplitz_table(codes):
    taps = codes.shape[2]
    rows = jnp.arange(2 * taps, dtype=jnp.int32)[:, None]
    cols = jnp.arange(taps, dtype=jnp.int32)[None, :]
    offset = rows - cols
    inside = (offset >= 0) & (offset < taps)
    clipped = jnp.clip(offset, 0, taps - 1)
    in_phase = jnp.where(inside[None], codes[:, 0, :][:, clipped], 0.0)
    quadrature = jnp.where(inside[None], codes[:, 1, :][:, clipped], 0.0)
    return jnp.concatenate([in_phase, quadrature], axis=2)


def hadamard_signs(order, columns, emissions):
    parity = jnp.zeros((order.shape[0], columns.shape[0]), jnp.int32)
    for bit in range(emissions.bit_length()):
        parity = parity + (order[:, None] >> bit & columns[None, :] >> bit & 1)
    signs = (1 - 2 * (parity % 2)).astype(jnp.float32)
    return signs / jnp.sqrt(jnp.float32(emissions))


def spectral_table(samples, taps, bins):
    rows = jnp.arange(samples // taps * 2 * taps, dtype=jnp.int32)
    block = rows // (2 * taps)
    quad = rows // taps % 2
    sample = block * taps + rows % taps
    freqs = jnp.arange(bins, dtype=jnp.int32) - bins // 2
    phase = jnp.mod(sample[:, None] * freqs[None, :], samples).astype(jnp.float32)
    angle = phase * (2.0 * jnp.pi / samples)
    cosine = jnp.cos(angle)
    sine = jnp.sin(angle)
    is_quad = quad[:, None] == 1
    real_cols = jnp.where(is_quad, sine, cosine)
    imag_cols = jnp.where(is_quad, cosine, -sine)
    return jnp.concatenate([real_cols, imag_cols], axis=1) / jnp.sqrt(jnp.float32(samples))


def steer_bins(source, steer, count, contract):
    bins = steer.shape[0]
    half = steer.shape[2] // 2
    real_part = lax.slice_in_dim(source, 0, count, axis=0)
    imag_part = lax.dynamic_slice_in_dim(source, bins, count, 0)
    numbers = (((contract,), (1,)), ((0,), (0,)))
    first = lax.dot_general(real_part, steer, numbers, precision=lax.Precision.HIGHEST)
    second = lax.dot_general(imag_part, steer, numbers, precision=lax.Precision.HIGHEST)
    return jnp.concatenate(
        [first[..., :half] - second[..., half:], first[..., half:] + second[..., :half]], axis=2
    )


def per_device(traces, codes, code_of, order, steer):
    edev, mdev, samples = traces.shape
    ncode, taps = (codes.shape[0], codes.shape[2])
    emissions = order.shape[0]
    bins = steer.shape[0]
    bins_dev = bins // lax.axis_size("elem")
    nblock = samples // taps
    first = lax.axis_index("emit") * edev
    own_codes = lax.dynamic_slice_in_dim(code_of, first, edev)
    onehot = (own_codes[:, None] == jnp.arange(ncode, dtype=jnp.int32)[None, :]).astype(jnp.float32)
    table = toeplitz_table(codes)
    picked = jnp.einsum("ec,cjd->ejd", onehot, table, precision=lax.Precision.HIGHEST)
    blocks = traces.reshape(edev, mdev, nblock, taps)
    current = jnp.einsum(
        "emnj,ejd->emnd", blocks, picked[:, :taps, :], precision=lax.Precision.HIGHEST
    )
    following = jnp.einsum(
        "emnj,ejd->emnd", blocks, picked[:, taps:, :], precision=lax.Precision.HIGHEST
    )
    following = jnp.concatenate(
        [following[:, :, 1:], jnp.zeros((edev, mdev, 1, 2 * taps), jnp.float32)], axis=2
    )
    corr = (current + following).reshape(edev, mdev, nblock * 2 * taps)
    transform = spectral_table(samples, taps, bins)
    spectra = lax.dot_general(
        transform, corr, (((0,), (2,)), ((), ())), precision=lax.Precision.HIGHEST
    )
    columns = first + jnp.arange(edev, dtype=jnp.int32)
    hadamard = hadamard_signs(order, columns, emissions)
    decoded = lax.dot_general(
        lax.all_gather(spectra, "emit", axis=1, tiled=True),
        hadamard,
        (((1,), (0,)), ((), ())),
        precision=lax.Precision.HIGHEST,
    )
    return lax.psum_scatter(
        steer_bins(decoded, steer, bins_dev * lax.axis_size("elem"), 1),
        "elem",
        scatter_dimension=0,
        tiled=True,
    )


def solution(mesh):
    placed = (P("emit", "elem", None), P(), P(), P(), P(None, "elem", None))
    return jax.shard_map(
        per_device, mesh=mesh, in_specs=placed, out_specs=P("elem", "emit", None), check_vma=False
    )
```

profile of v0, /device:TPU:0, one launch (start us, length us, event | category | flops | bytes accessed | tf_op | source)
XLA Modules:
  0.0 918.1 jit_solution(17875614214764076729)
XLA Ops:
  6.5 0.0 all-gather.2.cloned.1.call-start
  6.5 0.1 fusion.23
  6.7 0.8 fusion.93
  7.5 0.1 copy.40
  7.6 108.5 %gather_fusion = f32[32768,4]{1,0:T(8,128)} fusion(f32[4,128]{0,1:T(8,128)S(1)} %bitcast.52, s32[32768]{0:T(1024)S(1)} %fusion.23), kind=kCustom, calls=%fused_computation | custom fusion | bytes 1179648 | tf_op jit(solution)/shard_map/gather | solution.py:14
  116.0 9.4 %copy.16 = f32[256,128,4]{1,2,0:T(4,128)S(1)} copy(f32[256,128,4]{2,1,0:T(8,128)} %bitcast.56) | data formatting | bytes 1048576 | tf_op jit(solution)/shard_map/gather | solution.py:14
  125.5 0.1 copy.41
  125.6 108.5 %gather_fusion.1 = f32[32768,4]{1,0:T(8,128)} fusion(f32[4,128]{0,1:T(8,128)S(1)} %bitcast.51, s32[32768]{0:T(1024)S(1)} %fusion.23), kind=kCustom, calls=%fused_computation.1 | custom fusion | bytes 1179648 | tf_op jit(solution)/shard_map/gather | solution.py:15
  234.1 0.0 copy-start.2
  234.1 9.4 %copy.19 = f32[256,128,4]{1,2,0:T(4,128)S(1)} copy(f32[256,128,4]{2,1,0:T(8,128)} %bitcast.55) | data formatting | bytes 1048576 | tf_op jit(solution)/shard_map/gather | solution.py:15
  243.5 0.0 copy-done.2
  243.5 0.1 dynamic_slice.6
  243.6 0.3 select_bitcast_fusion.1
  243.9 0.0 slice-start
  243.9 5.9 fusion.15
  249.8 0.0 slice-start.1
  249.8 6.8 slice_bitcast_fusion.1
  256.6 0.0 slice-done
  256.6 0.0 slice-done.1
  256.6 17.6 %convolution_bitcast_fusion = f32[32,64,8,256]{3,1,2,0:T(8,128)} fusion(f32[32,128,256,1]{2,0,1,3:T(8,128)S(1)} %get-tuple-element.8, f32[32,64,1024]{2,1,0:T(8,128)S(1)} %bitcast.54), kind=kOutput, calls=%fused_computation.3 | convolution fusion | flops 6442450944 | bytes 29360128 | tf_op jit(solution)/shard_map/emnj,ejd->emnd/dot_general | solution.py:72
  274.2 13.1 %slice.46 = f32[32,64,7,256]{3,1,2,0:T(8,128)} slice(f32[32,64,8,256]{3,1,2,0:T(8,128)} %convolution_bitcast_fusion), slice={[0:32], [0:64], [1:8], [0:256]} | slice | bytes 29360128 | tf_op jit(solution)/shard_map/slice | solution.py:76
  287.3 29.1 %bitcast_add_fusion = f32[32,64,8,256]{3,1,2,0:T(8,128)} fusion(f32[32,64,7,256]{3,1,2,0:T(8,128)} %slice.46, f32[32,128,256,1]{2,0,1,3:T(8,128)} %get-tuple-element.7, f32[32,64,1024]{2,1,0:T(8,128)} %param.5), kind=kOutput, calls=%fused_computation.2 | convolution fusion | flops 6446645248 | bytes 44040192 | tf_op jit(solution)/shard_map/emnj,ejd->emnd/dot_general | solution.py:69
  316.4 18.2 %copy.38 = f32[32,64,8,256]{3,2,0,1:T(8,128)} copy(f32[32,64,8,256]{3,1,2,0:T(8,128)} %bitcast_add_fusion) | data formatting | bytes 33554432 | tf_op jit(solution)/shard_map/reshape | solution.py:78
  334.6 18.0 %reshape.181 = f32[32,64,2048]{2,0,1:T(8,128)} reshape(f32[32,64,8,256]{3,2,0,1:T(8,128)} %copy.38) | data formatting | bytes 33554432 | tf_op jit(solution)/shard_map/reshape | solution.py:78
  352.5 8.5 fusion.21
  361.1 30.8 %fusion.5 = f32[512,32,64]{0,1,2:T(8,128)} fusion(f32[32,64,2048]{2,0,1:T(8,128)} %reshape.181, f32[2048,256]{1,0:T(8,128)S(1)} %get-tuple-element.14, f32[2048,256]{1,0:T(8,128)S(1)} %get-tuple-element.13), kind=kOutput, calls=%fused_computation.15 | convolution fusion | flops 25771900928 | bytes 25165824 | tf_op jit(solution)/shard_map/dot_general | solution.py:80
  391.8 0.0 copy-start.1
  391.8 0.0 all-gather.2.cloned.1.call-update
  391.9 0.0 reduce-scatter.2.cloned.1.call-start
  392.0 0.5 copy-done.1
  392.5 336.3 %all-gather.2.cloned.1.call-done = f32[512,256,64]{0,1,2:T(8,128)} async-done(((f32[512,32,64]{0,1,2:T(8,128)}), f32[512,256,64]{0,1,2:T(8,128)}) %all-gather.2.cloned.1.call-update) | async-done | bytes 33554448 | tf_op jit(solution)/shard_map/all_gather | solution.py:86
  728.8 25.7 %fusion.33 = f32[512,64,32]{0,2,1:T(8,128)} fusion(f32[512,256,64]{0,1,2:T(8,128)} %all-gather.2.cloned.1.call-done, s32[32]{0:T(128)S(1)} %get-tuple-element.26, s32[256]{0:T(256)S(1)} %get-tuple-element.24, s32[32]{0:T(128)S(1)} %get-tuple-element.27, s32[256]{0:T(256)S(1)} %get-tuple-element.25, s32[32]{0:T(128)S(1)} %get-tuple-element.28, ...), kind=kOutput, calls=%fused_computation.55 | convolution fusion | flops 3221561344 | bytes 37759104 | tf_op jit(solution)/shard_map/dot_general | solution.py:85
  754.6 4.0 fusion.92
  758.6 5.6 copy.25
  764.2 4.5 copy.26
  768.6 0.0 copy-start
  768.7 16.0 %fusion.94 = f32[256,32,256]{2,1,0:T(8,128)} fusion(f32[256,64,32]{1,2,0:T(8,128)} %copy.25, f32[256,64,256]{2,1,0:T(8,128)} %param.9), kind=kOutput, calls=%fused_computation.136 | convolution fusion | flops 1610612736 | bytes 27262976 | tf_op jit(solution)/shard_map/dot_general | solution.py:49
  784.7 0.0 copy-done
  784.7 14.1 %fusion.95 = f32[256,32,256]{2,1,0:T(8,128)} fusion(f32[256,64,32]{1,2,0:T(8,128)S(1)} %copy-done, f32[256,64,256]{2,1,0:T(8,128)} %param.9), kind=kOutput, calls=%fused_computation.137 | convolution fusion | flops 1610612736 | bytes 27262976 | tf_op jit(solution)/shard_map/dot_general | solution.py:50
  798.8 9.9 %slice_subtract_fusion = (f32[256,32,128]{2,1,0:T(8,128)S(1)}, f32[256,32,128]{2,1,0:T(8,128)}) fusion(f32[256,32,256]{2,1,0:T(8,128)} %fusion.95, f32[256,32,256]{2,1,0:T(8,128)} %fusion.94), kind=kLoop, calls=%fused_computation.10 | loop fusion | flops 2097152 | bytes 25165824 | tf_op jit(solution)/shard_map/sub | solution.py:52
  808.7 6.4 pad_maximum_fusion
  815.1 0.0 reduce-scatter.2.cloned.1.call-update
  815.1 95.7 %reduce-scatter.2.cloned.1.call-done = f32[16,32,256]{2,1,0:T(8,128)} async-done(((f32[256,32,256]{2,1,0:T(8,128)}), f32[16,32,256]{2,1,0:T(8,128)}) %reduce-scatter.2.cloned.1.call-update) | async-done | bytes 524304 | tf_op jit(solution)/shard_map/reduce_scatter | solution.py:91
  (11 shorter events, 0.1 us)
Async XLA Ops:
  6.5 722.3 %all-gather.2.cloned.1.call-start = ((), (), s32[]{:S(2)}) async-start(), calls=%async_computation.1 | async-start | bytes 37748736 | tf_op jit(solution)/shard_map/all_gather | solution.py:86
  234.1 9.4 %copy-start.2 = (s32[256]{0:T(256)S(1)}, s32[256]{0:T(256)}, u32[]{:S(2)}) copy-start(s32[256]{0:T(256)} %param.7) | copy-start | bytes 3076
  243.9 12.7 %slice-start = ((s8[8388608]{0:T(1024)(128)(4,1)}), s8[4194304]{0:T(1024)(128)(4,1)S(1)}, s32[]{:S(2)}) async-start(s8[8388608]{0:T(1024)(128)(4,1)} %bitcast.53), calls=%async_computation.3 | async-start | bytes 8388608
  249.8 6.8 slice-start.1
  391.8 0.7 copy-start.1
  391.9 518.9 %reduce-scatter.2.cloned.1.call-start = ((), (), s32[]{:S(2)}) async-start(), calls=%async_computation.2 | async-start | bytes 8912896 | tf_op jit(solution)/shard_map/reduce_scatter | solution.py:91
  768.6 16.0 %copy-start = (f32[256,64,32]{1,2,0:T(8,128)S(1)}, f32[256,64,32]{1,2,0:T(8,128)}, u32[]{:S(2)}) copy-start(f32[256,64,32]{1,2,0:T(8,128)} %copy.26) | copy-start | bytes 6291460
Sparse Core Ops, SparseCore 0:
  392.0 336.7 all-gather.1
  815.2 95.5 reduce-scatter.1
where the time goes:
time: 926 us; the launch traced here: 918 us
  waiting for transfers between devices  432 us (47%)
  local copies, waits for them, and re-layouts  308 us (33%)
  matrix products  139 us (15%)
  other arithmetic  25.2 us (3%)
  between operations  14 us (2%)
    all_gather x1, waiting for transfers between devices, per_device(): lax.all_gather(spectra, 'emit', axis=1, tiled=True)  336 us
    gather x2, local copies, waits for them, and re-layouts, toeplitz_table(): quadrature = jnp.where(inside[None], codes[:, 1, :][:, clipped], 0.0)  118 us
    gather x2, local copies, waits for them, and re-layouts, toeplitz_table(): in_phase = jnp.where(inside[None], codes[:, 0, :][:, clipped], 0.0)  118 us
    reduce_scatter x1, waiting for transfers between devices, per_device(): lax.psum_scatter(steer_bins(decoded, steer, bins_dev * lax.axis_size('ele...  95.7 us
    reshape x2, local copies, waits for them, and re-layouts, per_device(): corr = (current + following).reshape(edev, mdev, nblock * 2 * taps)  36.1 us
    dot_general x1, matrix products, per_device(): lax.dot_general(transform, corr, (((0,), (2,)), ((), ())), precision=lax....  30.8 us
    dot_general x1, matrix products, per_device(): jnp.einsum('emnj,ejd->emnd', blocks, picked[:, :taps, :], precision=lax.P...  29.1 us
    dot_general x1, matrix products, per_device(): lax.dot_general(lax.all_gather(spectra, 'emit', axis=1, tiled=True), hada...  25.7 us
  transfers between devices with their start and end apart: 2, of which 2 were waited for; matrix products, arithmetic and copies ran while one was open for 0% of the time, Pallas kernels for 0%

commit v1 on v0

--- a/solution.py
+++ b/solution.py
@@ -83,7 +83,9 @@
     columns = first + jnp.arange(edev, dtype=jnp.int32)
     hadamard = hadamard_signs(order, columns, emissions)
     decoded = lax.dot_general(
-        lax.all_gather(spectra, "emit", axis=1, tiled=True),
+        jnp.concatenate(
+            lax.all_to_all(jnp.stack([spectra] * lax.axis_size("emit")), "emit", 0, 0), axis=1
+        ),
         hadamard,
         (((1,), (0,)), ((), ())),
         precision=lax.Precision.HIGHEST,

time: 926 us -> 963 us (1.040)
  waiting for transfers between devices: 432 us -> 461 us
  matrix products: 139 us -> 156 us
  local copies, waits for them, and re-layouts: 308 us -> 291 us
    all_to_all x0 -> x1, waiting for transfers between devices: none -> 364 us  [per_device(): lax.all_to_all(jnp.stack([spectra] * lax.axis_size('emit')), 'emit', 0, 0)]
    all_gather x1 -> x0, waiting for transfers between devices: 336 us -> none  [per_device(): lax.all_gather(spectra, 'emit', axis=1, tiled=True)]
    reshape x2 -> x1, local copies, waits for them, and re-layouts: 36.1 us -> 7.58 us  [per_device(): corr = (current + following).reshape(edev, mdev, nblock * 2 * taps)]
    dot_general x1, matrix products: 25.7 us -> 45.2 us  [per_device(): lax.dot_general(jnp.concatenate(lax.all_to_all(jnp.stack([spectra] * lax....]
    another operation x0 -> x1, local copies, waits for them, and re-layouts: none -> 11.4 us  [per_device(): jnp.stack([spectra] * lax.axis_size('emit'))]
where the time goes in v1:
time: 963 us; the launch traced here: 956 us
  waiting for transfers between devices  461 us (48%)
  local copies, waits for them, and re-layouts  291 us (30%)
  matrix products  156 us (16%)
  other arithmetic  25.2 us (3%)
  between operations  14.1 us (1%)
    all_to_all x1, waiting for transfers between devices, per_device(): lax.all_to_all(jnp.stack([spectra] * lax.axis_size('emit')), 'emit', 0, 0)  364 us
    gather x2, local copies, waits for them, and re-layouts, toeplitz_table(): quadrature = jnp.where(inside[None], codes[:, 1, :][:, clipped], 0.0)  118 us
    gather x2, local copies, waits for them, and re-layouts, toeplitz_table(): in_phase = jnp.where(inside[None], codes[:, 0, :][:, clipped], 0.0)  118 us
    reduce_scatter x1, waiting for transfers between devices, per_device(): lax.psum_scatter(steer_bins(decoded, steer, bins_dev * lax.axis_size('ele...  97.5 us
    dot_general x1, matrix products, per_device(): lax.dot_general(jnp.concatenate(lax.all_to_all(jnp.stack([spectra] * lax....  45.2 us
    dot_general x1, matrix products, per_device(): jnp.einsum('emnj,ejd->emnd', blocks, picked[:, :taps, :], precision=lax.P...  29.2 us
    dot_general x1, matrix products, per_device(): lax.dot_general(transform, corr, (((0,), (2,)), ((), ())), precision=lax....  28.1 us
  transfers between devices with their start and end apart: 2, of which 2 were waited for; matrix products, arithmetic and copies ran while one was open for 0% of the time, Pallas kernels for 0%

profile of v1, /device:TPU:0, one launch (start us, length us, event | category | flops | bytes accessed | tf_op | source)
XLA Modules:
  0.0 955.7 jit_solution(10511183601115813765)
XLA Ops:
  6.5 0.1 fusion.26
  6.7 0.8 fusion.95
  7.4 0.1 copy.39
  7.6 109.0 %gather_fusion = f32[32768,4]{1,0:T(8,128)} fusion(f32[4,128]{0,1:T(8,128)S(1)} %bitcast.55, s32[32768]{0:T(1024)S(1)} %fusion.26), kind=kCustom, calls=%fused_computation | custom fusion | bytes 1179648 | tf_op jit(solution)/shard_map/gather | solution.py:14
  116.6 9.4 copy.17
  126.0 0.1 copy.40
  126.1 109.0 %gather_fusion.1 = f32[32768,4]{1,0:T(8,128)} fusion(f32[4,128]{0,1:T(8,128)S(1)} %bitcast.54, s32[32768]{0:T(1024)S(1)} %fusion.26), kind=kCustom, calls=%fused_computation.1 | custom fusion | bytes 1179648 | tf_op jit(solution)/shard_map/gather | solution.py:15
  235.1 0.0 copy-start.2
  235.1 9.4 copy.20
  244.5 0.0 copy-done.2
  244.5 0.1 dynamic_slice.6
  244.6 0.3 select_bitcast_fusion.1
  244.9 0.0 slice-start
  244.9 5.9 fusion.18
  250.8 0.0 slice-start.1
  250.8 6.8 slice_bitcast_fusion.1
  257.6 0.0 slice-done
  257.6 0.0 slice-done.1
  257.6 17.7 %convolution_bitcast_fusion = f32[32,64,8,256]{3,1,2,0:T(8,128)} fusion(f32[32,128,256,1]{2,0,1,3:T(8,128)S(1)} %get-tuple-element.8, f32[32,64,1024]{2,1,0:T(8,128)S(1)} %bitcast.57), kind=kOutput, calls=%fused_computation.6 | convolution fusion | flops 6442450944 | bytes 29360128 | tf_op jit(solution)/shard_map/emnj,ejd->emnd/dot_general | solution.py:72
  275.3 13.1 %slice.46 = f32[32,64,7,256]{3,1,2,0:T(8,128)} slice(f32[32,64,8,256]{3,1,2,0:T(8,128)} %convolution_bitcast_fusion), slice={[0:32], [0:64], [1:8], [0:256]} | slice | bytes 29360128 | tf_op jit(solution)/shard_map/slice | solution.py:76
  288.4 29.2 %fusion.2 = f32[32,8,8,8,256]{4,3,2,1,0:T(8,128)} fusion(f32[32,64,7,256]{3,1,2,0:T(8,128)} %slice.46, f32[32,128,256,1]{2,0,1,3:T(8,128)} %get-tuple-element.7, f32[32,64,1024]{2,1,0:T(8,128)} %param.5), kind=kOutput, calls=%fused_computation.5 | convolution fusion | flops 6446645248 | bytes 44040192 | tf_op jit(solution)/shard_map/emnj,ejd->emnd/dot_general | solution.py:69
  317.6 7.6 copy.42
  325.2 8.5 fusion.24
  333.7 28.1 %fusion.8 = f32[512,32,64]{0,2,1:T(8,128)S(1)} fusion(f32[32,64,2048]{2,1,0:T(8,128)S(1)} %bitcast.60, f32[2048,256]{1,0:T(8,128)S(1)} %get-tuple-element.14, f32[2048,256]{1,0:T(8,128)S(1)} %get-tuple-element.13), kind=kOutput, calls=%fused_computation.18 | convolution fusion | flops 25771900928 | bytes 25165824 | tf_op jit(solution)/shard_map/dot_general | solution.py:80
  361.8 11.4 %stack.2 = f32[8,512,32,64]{1,3,2,0:T(8,128)} broadcast(f32[512,32,64]{0,2,1:T(8,128)S(1)} %fusion.8), dimensions={1,2,3} | broadcast | bytes 37748736 | tf_op jit(solution)/shard_map/stack | solution.py:87
  373.2 0.0 copy-start.1
  373.2 8.0 all-to-all-start
  381.2 0.0 reduce-scatter.2.cloned.1.call-start
  381.3 0.0 copy-done.1
  381.3 363.5 %all-to-all-done = f32[8,512,32,64]{1,3,2,0:T(8,128)} async-done(((f32[8,512,32,64]{1,3,2,0:T(8,128)}), f32[8,512,32,64]{1,3,2,0:T(8,128)}, u32[]{:S(2)}, u32[]{:S(2)}) %all-to-all-start) | async-done | bytes 33554464 | tf_op jit(solution)/shard_map/all_to_all | solution.py:87
  744.8 45.2 %fusion = f32[512,64,32]{0,2,1:T(8,128)} fusion(f32[512,256,64]{0,2,1:T(8,128)} %bitcast.14, s32[32]{0:T(128)S(1)} %get-tuple-element.26, s32[256]{0:T(256)S(1)} %get-tuple-element.24, s32[32]{0:T(128)S(1)} %get-tuple-element.27, s32[256]{0:T(256)S(1)} %get-tuple-element.25, s32[32]{0:T(128)S(1)} %get-tuple-element.28, s32[256]{0:T(256)S(1)} %get-tuple-element.18, ...), kind=kOutput, calls=%fused_computation.2 | convolution fusion | flops 3221561344 | bytes 37759104 | tf_op jit(solution)/shard_map/dot_general | solution.py:85
  790.0 4.0 fusion.94
  794.0 5.6 copy.27
  799.6 4.7 copy.28
  804.3 0.0 copy-start
  804.3 15.8 %fusion.96 = f32[256,32,256]{2,1,0:T(8,128)} fusion(f32[256,64,32]{1,2,0:T(8,128)} %copy.27, f32[256,64,256]{2,1,0:T(8,128)} %param.9), kind=kOutput, calls=%fused_computation.138 | convolution fusion | flops 1610612736 | bytes 27262976 | tf_op jit(solution)/shard_map/dot_general | solution.py:49
  820.1 0.0 copy-done
  820.1 14.3 %fusion.97 = f32[256,32,256]{2,1,0:T(8,128)} fusion(f32[256,64,32]{1,2,0:T(8,128)S(1)} %copy-done, f32[256,64,256]{2,1,0:T(8,128)} %param.9), kind=kOutput, calls=%fused_computation.139 | convolution fusion | flops 1610612736 | bytes 27262976 | tf_op jit(solution)/shard_map/dot_general | solution.py:50
  834.5 9.9 %slice_subtract_fusion = (f32[256,32,128]{2,1,0:T(8,128)S(1)}, f32[256,32,128]{2,1,0:T(8,128)}) fusion(f32[256,32,256]{2,1,0:T(8,128)} %fusion.97, f32[256,32,256]{2,1,0:T(8,128)} %fusion.96), kind=kLoop, calls=%fused_computation.13 | loop fusion | flops 2097152 | bytes 25165824 | tf_op jit(solution)/shard_map/sub | solution.py:52
  844.4 6.4 pad_maximum_fusion
  850.7 0.0 reduce-scatter.2.cloned.1.call-update
  850.8 97.5 %reduce-scatter.2.cloned.1.call-done = f32[16,32,256]{2,1,0:T(8,128)} async-done(((f32[256,32,256]{2,1,0:T(8,128)}), f32[16,32,256]{2,1,0:T(8,128)}) %reduce-scatter.2.cloned.1.call-update) | async-done | bytes 524304 | tf_op jit(solution)/shard_map/reduce_scatter | solution.py:93
  (11 shorter events, 0.1 us)
Async XLA Ops:
  235.1 9.4 copy-start.2
  244.9 12.7 %slice-start = ((s8[8388608]{0:T(1024)(128)(4,1)}), s8[4194304]{0:T(1024)(128)(4,1)S(1)}, s32[]{:S(2)}) async-start(s8[8388608]{0:T(1024)(128)(4,1)} %bitcast.56), calls=%async_computation.3 | async-start | bytes 8388608
  250.8 6.8 slice-start.1
  373.2 8.1 copy-start.1
  373.2 371.6 %all-to-all-start = ((f32[8,512,32,64]{1,3,2,0:T(8,128)}), f32[8,512,32,64]{1,3,2,0:T(8,128)}, u32[]{:S(2)}, u32[]{:S(2)}) async-start(f32[8,512,32,64]{1,3,2,0:T(8,128)} %stack.2), calls=%async_computation | async-start | bytes 67108864 | tf_op jit(solution)/shard_map/all_to_all | solution.py:87
  381.2 567.1 %reduce-scatter.2.cloned.1.call-start = ((), (), s32[]{:S(2)}) async-start(), calls=%async_computation.2 | async-start | bytes 8912896 | tf_op jit(solution)/shard_map/reduce_scatter | solution.py:93
  804.3 15.8 %copy-start = (f32[256,64,32]{1,2,0:T(8,128)S(1)}, f32[256,64,32]{1,2,0:T(8,128)}, u32[]{:S(2)}) copy-start(f32[256,64,32]{1,2,0:T(8,128)} %copy.28) | copy-start | bytes 6291460
Sparse Core Ops, SparseCore 0:
  850.9 97.3 reduce-scatter.1
